TPU v7x, 32 devices: a whole 2x2x4 slice. The times are simulated.
32 devices in a mesh: tm: 4 (over x, core), rows: 8 (over z, y).
Axes of the slice: x: 2, y: 2, z: 4, core: 2. Of those that a mesh axis runs over, the one named last changes fastest.
Arguments:
- latent_feat: bfloat16 [16, 16, 128, 384], P('tm', 'rows'), may hold values from -6 to 6
- norm_gain: float32 [384], replicated, may hold values from 0.25 to 1.75
- conv_weight: bfloat16 [27, 384, 384], replicated, may hold values from -0.0625 to 0.0625
- rgb_weight: bfloat16 [384, 3], replicated, may hold values from -0.3125 to 0.3125
- real_frames: bfloat16 [3, 16, 16, 128], P(None, 'tm', 'rows'), may hold values from -6 to 6
- disc_first: bfloat16 [27, 64, 3], replicated, may hold values from -0.625 to 0.625
- disc_second: bfloat16 [27, 128, 64], replicated, may hold values from -0.15625 to 0.15625
Outputs:
- decoded: bfloat16 [16, 16, 128, 384], P('tm', 'rows')
- match_map: float32 [16, 16, 128], P('tm', 'rows')
All inputs are finite; a program needn't handle non-finite values.
Results may differ from a plain program's by a relative error of at most 0.0033.
Values may be sent and summed in bfloat16 or wider, within the bound.
A program may use at most 128 MiB of HBM per device.

v0:
```python
import jax
import jax.numpy as jnp
from jax import lax
from jax.sharding import PartitionSpec as P


def from_behind(block, axis, distance):
    devices = range(lax.axis_size(axis))
    route = [(i - distance, i) for i in devices if i - distance in devices]
    return lax.ppermute(block, axis, route)


def extended_2(cells, sides, width):
    for axis, dim in sides:
        count = lax.axis_size(axis)
        ends = count - 1
        head = lax.slice_in_dim(cells, 0, width, axis=dim)
        tail = lax.slice_in_dim(cells, cells.shape[dim] - width, cells.shape[dim], axis=dim)
        cells = jnp.concatenate(
            [
                lax.ppermute(tail, axis, [(i, (i + 1) % count) for i in range(ends)]),
                cells,
                lax.ppermute(head, axis, [((i + 1) % count, i) for i in range(ends)]),
            ],
            axis=dim,
        )
    return cells


def leaky(value):
    return jnp.maximum(value, 0.2 * value)


def conv_valid(extended, weights):
    frames = extended.shape[1] - 2
    height = extended.shape[2] - 2
    width = extended.shape[3] - 2
    total = jnp.zeros((weights.shape[1], frames, height, width), jnp.float32)
    for tap in range(27):
        dt, dh, dw = (tap // 9, tap // 3 % 3, tap % 3)
        piece = extended[:, dt : dt + frames, dh : dh + height, dw : dw + width]
        total = total + jnp.einsum(
            "oc,cthw->othw", weights[tap], piece, preferred_element_type=jnp.float32
        )
    return leaky(total)


def per_device(
    latent_feat, norm_gain, conv_weight, rgb_weight, real_frames, disc_first, disc_second
):
    feats = latent_feat.astype(jnp.float32)
    normed = feats * lax.rsqrt(jnp.mean(feats * feats, axis=-1, keepdims=True) + 1e-06) * norm_gain
    act = jax.nn.silu(normed).astype(jnp.bfloat16)
    frames, height, width, chans = act.shape
    cached = from_behind(act[frames - 2 :], "tm", 1)
    extended = jnp.concatenate([cached, act], axis=0)
    extended = extended_2(extended, (("rows", 1),), 1)
    extended = jnp.pad(extended, ((0, 0), (0, 0), (1, 1), (0, 0)))
    total = jnp.zeros((frames * height * width, chans), jnp.float32)
    for tap in range(27):
        dt, dh, dw = (tap // 9, tap // 3 % 3, tap % 3)
        piece = extended[dt : dt + frames, dh : dh + height, dw : dw + width].reshape(-1, chans)
        total = total + jnp.dot(piece, conv_weight[tap], preferred_element_type=jnp.float32)
    decoded = (feats + total.reshape(frames, height, width, chans)).astype(jnp.bfloat16)
    colour = jnp.dot(
        decoded.reshape(-1, chans), rgb_weight, preferred_element_type=jnp.float32
    ).astype(jnp.bfloat16)
    fake = jnp.transpose(colour.reshape(frames, height, width, 3), (3, 0, 1, 2))
    stacked = jnp.concatenate([fake, real_frames], axis=0)
    ext_in = extended_2(stacked, (("tm", 1), ("rows", 2)), 1)
    ext_in = jnp.pad(ext_in, ((0, 0), (0, 0), (0, 0), (1, 1)))
    first_fake = conv_valid(ext_in[:3], disc_first).astype(jnp.bfloat16)
    first_real = conv_valid(ext_in[3:], disc_first).astype(jnp.bfloat16)
    both_first = jnp.concatenate([first_fake, first_real], axis=0)
    ext_mid = extended_2(both_first, (("tm", 1), ("rows", 2)), 1)
    ext_mid = jnp.pad(ext_mid, ((0, 0), (0, 0), (0, 0), (1, 1)))
    depth = first_fake.shape[0]
    second_fake = conv_valid(ext_mid[:depth], disc_second).astype(jnp.bfloat16)
    second_real = conv_valid(ext_mid[depth:], disc_second).astype(jnp.bfloat16)
    match_map = jnp.mean(
        jnp.abs(first_fake.astype(jnp.float32) - first_real.astype(jnp.float32)), axis=0
    )
    match_map = match_map + jnp.mean(
        jnp.abs(second_fake.astype(jnp.float32) - second_real.astype(jnp.float32)), axis=0
    )
    return (decoded, match_map)


def solution(mesh):
    placed = (P("tm", "rows", None, None), P(), P(), P(), P(None, "tm", "rows", None), P(), P())
    return jax.shard_map(
        per_device,
        mesh=mesh,
        in_specs=placed,
        out_specs=(P("tm", "rows", None, None), P("tm", "rows", None)),
        check_vma=False,
    )
```

profile of v0, /device:TPU:0, one launch (start us, length us, event | category | flops | bytes accessed | tf_op | source)
XLA Modules:
  0.0 168.7 jit_solution(2270623910806346300)
XLA Ops:
  0.7 1.4 fusion.5
  2.1 1.7 fusion.12
  3.8 2.8 %collective-permute-start = (bf16[2,2,128,384]{3,2,1,0:T(8,128)(2,1)S(1)}, bf16[2,2,128,384]{3,2,1,0:T(8,128)(2,1)S(1)}, u32[]{:S(2)}, u32[]{:S(2)}) collective-permute-start(bf16[2,2,128,384]{3,2,1,0:T(8,128)(2,1)S(1)} %slice.1161), channel_id=1, source_target_pairs={{0,8},{8,16},{16,24},{1,9},{9,17},{17,25},{2,10},{10,18},{18,26},{... | collective-permute-start | bytes 1179656 | tf_op jit(solution)/shard_map/ppermute | solution.py:10
  6.7 1.6 fusion.121
  8.4 4.3 %collective-permute-start.1 = (bf16[6,1,128,384]{3,2,1,0:T(8,128)(2,1)S(1)}, bf16[6,1,128,384]{3,2,1,0:T(8,128)(2,1)S(1)}, u32[]{:S(2)}, u32[]{:S(2)}) collective-permute-start(bf16[6,1,128,384]{3,2,1,0:T(8,128)(2,1)S(1)} %get-tuple-element.30), channel_id=1, source_target_pairs={{0,1},{1,2},{2,3},{3,4},{4,5},{5,6},{6,7},{8,9},{9,10},{10,11},{11... | collective-permute-start | bytes 1769480 | tf_op jit(solution)/shard_map/ppermute | solution.py:21
  12.7 1.3 collective-permute-start.2
  14.2 1.8 %fusion.139 = f32[1024,384]{1,0:T(8,128)} fusion(bf16[1024,384]{1,0:T(8,128)(2,1)S(1)} %bitcast.836, bf16[27,384,384]{2,1,0:T(8,128)(2,1)S(1)} %copy-done.1), kind=kOutput, calls=%fused_computation.240 | convolution fusion | flops 301989888 | bytes 2654208 | tf_op jit(solution)/shard_map/dot_general | solution.py:63
  16.0 1.8 %fusion.157 = f32[1024,384]{1,0:T(8,128)} fusion(bf16[1024,384]{1,0:T(8,128)(2,1)S(1)} %bitcast.835, bf16[27,384,384]{2,1,0:T(8,128)(2,1)S(1)} %copy-done.1), kind=kOutput, calls=%fused_computation.258 | convolution fusion | flops 301989888 | bytes 2654208 | tf_op jit(solution)/shard_map/dot_general | solution.py:63
  17.8 17.5 %collective-permute-done.1 = bf16[6,1,128,384]{3,2,1,0:T(8,128)(2,1)S(1)} collective-permute-done((bf16[6,1,128,384]{3,2,1,0:T(8,128)(2,1)S(1)}, bf16[6,1,128,384]{3,2,1,0:T(8,128)(2,1)S(1)}, u32[]{:S(2)}, u32[]{:S(2)}) %collective-permute-start.1) | collective-permute-done | bytes 589856 | tf_op jit(solution)/shard_map/ppermute | solution.py:21
  36.5 1.8 %fusion.115 = f32[1024,384]{1,0:T(8,128)} fusion(bf16[1024,384]{1,0:T(8,128)(2,1)S(1)} %bitcast.834, bf16[27,384,384]{2,1,0:T(8,128)(2,1)S(1)} %copy-done.1), kind=kOutput, calls=%fused_computation.216 | convolution fusion | flops 301989888 | bytes 2654208 | tf_op jit(solution)/shard_map/dot_general | solution.py:63
  38.3 1.9 %fusion.127 = f32[1024,384]{1,0:T(8,128)} fusion(bf16[1024,384]{1,0:T(8,128)(2,1)S(1)} %bitcast.833, bf16[27,384,384]{2,1,0:T(8,128)(2,1)S(1)} %copy-done.1), kind=kOutput, calls=%fused_computation.228 | convolution fusion | flops 301989888 | bytes 2654208 | tf_op jit(solution)/shard_map/dot_general | solution.py:63
  40.2 1.8 %fusion.133 = f32[1024,384]{1,0:T(8,128)} fusion(bf16[1024,384]{1,0:T(8,128)(2,1)S(1)} %bitcast.832, bf16[27,384,384]{2,1,0:T(8,128)(2,1)S(1)} %copy-done.1), kind=kOutput, calls=%fused_computation.234 | convolution fusion | flops 301989888 | bytes 2654208 | tf_op jit(solution)/shard_map/dot_general | solution.py:63
  42.0 1.8 %fusion.145 = f32[1024,384]{1,0:T(8,128)} fusion(bf16[1024,384]{1,0:T(8,128)(2,1)S(1)} %bitcast.831, bf16[27,384,384]{2,1,0:T(8,128)(2,1)S(1)} %copy-done.1), kind=kOutput, calls=%fused_computation.246 | convolution fusion | flops 301989888 | bytes 2654208 | tf_op jit(solution)/shard_map/dot_general | solution.py:63
  43.8 1.8 %fusion.151 = f32[1024,384]{1,0:T(8,128)} fusion(bf16[1024,384]{1,0:T(8,128)(2,1)S(1)} %bitcast.830, bf16[27,384,384]{2,1,0:T(8,128)(2,1)S(1)} %copy-done.1), kind=kOutput, calls=%fused_computation.252 | convolution fusion | flops 301989888 | bytes 2654208 | tf_op jit(solution)/shard_map/dot_general | solution.py:63
  45.5 1.8 %fusion.163 = f32[1024,384]{1,0:T(8,128)} fusion(bf16[1024,384]{1,0:T(8,128)(2,1)S(1)} %bitcast.829, bf16[27,384,384]{2,1,0:T(8,128)(2,1)S(1)} %copy-done.1), kind=kOutput, calls=%fused_computation.264 | convolution fusion | flops 301989888 | bytes 2654208 | tf_op jit(solution)/shard_map/dot_general | solution.py:63
  47.3 1.4 select_maximum_fusion
  48.8 3.4 %fusion.477 = (bf16[4,2,128,384]{3,2,1,0:T(8,128)(2,1)S(1)}, bf16[4,2,128,384]{3,2,1,0:T(8,128)(2,1)S(1)}, bf16[4,2,128,384]{3,2,1,0:T(8,128)(2,1)S(1)}, bf16[4,...) fusion(bf16[6,4,130,384]{3,2,1,0:T(8,128)(2,1)S(1)} %select_max, ...), kind=kLoop, calls=%fused_computation.625 | loop fusion | bytes 28311552 | tf_op jit(solution)/shard_map/slice | solution.py:62
  52.2 1.8 %fusion.117 = f32[1024,384]{1,0:T(8,128)} fusion(bf16[1024,384]{1,0:T(8,128)(2,1)S(1)} %bitcast.826, bf16[27,384,384]{2,1,0:T(8,128)(2,1)S(1)} %copy-done.1), kind=kOutput, calls=%fused_computation.218 | convolution fusion | flops 301989888 | bytes 2654208 | tf_op jit(solution)/shard_map/dot_general | solution.py:63
  53.9 1.8 %fusion.119 = f32[1024,384]{1,0:T(8,128)} fusion(bf16[1024,384]{1,0:T(8,128)(2,1)S(1)} %bitcast.825, bf16[27,384,384]{2,1,0:T(8,128)(2,1)S(1)} %copy-done.1), kind=kOutput, calls=%fused_computation.220 | convolution fusion | flops 301989888 | bytes 2654208 | tf_op jit(solution)/shard_map/dot_general | solution.py:63
  55.7 1.8 %fusion.123 = f32[1024,384]{1,0:T(8,128)} fusion(bf16[1024,384]{1,0:T(8,128)(2,1)S(1)} %bitcast.824, bf16[27,384,384]{2,1,0:T(8,128)(2,1)S(1)} %copy-done.1), kind=kOutput, calls=%fused_computation.224 | convolution fusion | flops 301989888 | bytes 2654208 | tf_op jit(solution)/shard_map/dot_general | solution.py:63
  57.5 1.8 %fusion.125 = f32[1024,384]{1,0:T(8,128)} fusion(bf16[1024,384]{1,0:T(8,128)(2,1)S(1)} %bitcast.823, bf16[27,384,384]{2,1,0:T(8,128)(2,1)S(1)} %copy-done.1), kind=kOutput, calls=%fused_computation.226 | convolution fusion | flops 301989888 | bytes 2654208 | tf_op jit(solution)/shard_map/dot_general | solution.py:63
  59.3 1.8 %fusion.129 = f32[1024,384]{1,0:T(8,128)} fusion(bf16[1024,384]{1,0:T(8,128)(2,1)S(1)} %bitcast.822, bf16[27,384,384]{2,1,0:T(8,128)(2,1)S(1)} %copy-done.1), kind=kOutput, calls=%fused_computation.230 | convolution fusion | flops 301989888 | bytes 2654208 | tf_op jit(solution)/shard_map/dot_general | solution.py:63
  61.0 1.8 %fusion.131 = f32[1024,384]{1,0:T(8,128)} fusion(bf16[1024,384]{1,0:T(8,128)(2,1)S(1)} %bitcast.821, bf16[27,384,384]{2,1,0:T(8,128)(2,1)S(1)} %copy-done.1), kind=kOutput, calls=%fused_computation.232 | convolution fusion | flops 301989888 | bytes 2654208 | tf_op jit(solution)/shard_map/dot_general | solution.py:63
  62.9 1.8 %fusion.135 = f32[1024,384]{1,0:T(8,128)} fusion(bf16[1024,384]{1,0:T(8,128)(2,1)S(1)} %bitcast.820, bf16[27,384,384]{2,1,0:T(8,128)(2,1)S(1)} %copy-done.1), kind=kOutput, calls=%fused_computation.236 | convolution fusion | flops 301989888 | bytes 2654208 | tf_op jit(solution)/shard_map/dot_general | solution.py:63
  64.6 1.8 %fusion.137 = f32[1024,384]{1,0:T(8,128)} fusion(bf16[1024,384]{1,0:T(8,128)(2,1)S(1)} %bitcast.819, bf16[27,384,384]{2,1,0:T(8,128)(2,1)S(1)} %copy-done.1), kind=kOutput, calls=%fused_computation.238 | convolution fusion | flops 301989888 | bytes 2654208 | tf_op jit(solution)/shard_map/dot_general | solution.py:63
  66.4 1.8 %fusion.141 = f32[1024,384]{1,0:T(8,128)} fusion(bf16[1024,384]{1,0:T(8,128)(2,1)S(1)} %bitcast.818, bf16[27,384,384]{2,1,0:T(8,128)(2,1)S(1)} %copy-done.1), kind=kOutput, calls=%fused_computation.242 | convolution fusion | flops 301989888 | bytes 2654208 | tf_op jit(solution)/shard_map/dot_general | solution.py:63
  68.2 1.8 %fusion.143 = f32[1024,384]{1,0:T(8,128)} fusion(bf16[1024,384]{1,0:T(8,128)(2,1)S(1)} %bitcast.817, bf16[27,384,384]{2,1,0:T(8,128)(2,1)S(1)} %copy-done.1), kind=kOutput, calls=%fused_computation.244 | convolution fusion | flops 301989888 | bytes 2654208 | tf_op jit(solution)/shard_map/dot_general | solution.py:63
  70.0 1.8 %fusion.147 = f32[1024,384]{1,0:T(8,128)} fusion(bf16[1024,384]{1,0:T(8,128)(2,1)S(1)} %bitcast.816, bf16[27,384,384]{2,1,0:T(8,128)(2,1)S(1)} %copy-done.1), kind=kOutput, calls=%fused_computation.248 | convolution fusion | flops 301989888 | bytes 2654208 | tf_op jit(solution)/shard_map/dot_general | solution.py:63
  71.8 1.8 %fusion.149 = f32[1024,384]{1,0:T(8,128)} fusion(bf16[1024,384]{1,0:T(8,128)(2,1)S(1)} %bitcast.815, bf16[27,384,384]{2,1,0:T(8,128)(2,1)S(1)} %copy-done.1), kind=kOutput, calls=%fused_computation.250 | convolution fusion | flops 301989888 | bytes 2654208 | tf_op jit(solution)/shard_map/dot_general | solution.py:63
  73.7 1.9 %fusion.153 = f32[1024,384]{1,0:T(8,128)} fusion(bf16[1024,384]{1,0:T(8,128)(2,1)S(1)} %bitcast.814, bf16[27,384,384]{2,1,0:T(8,128)(2,1)S(1)} %copy-done.1), kind=kOutput, calls=%fused_computation.254 | convolution fusion | flops 301989888 | bytes 2654208 | tf_op jit(solution)/shard_map/dot_general | solution.py:63
  75.5 1.8 %fusion.155 = f32[1024,384]{1,0:T(8,128)} fusion(bf16[1024,384]{1,0:T(8,128)(2,1)S(1)} %bitcast.813, bf16[27,384,384]{2,1,0:T(8,128)(2,1)S(1)} %copy-done.1), kind=kOutput, calls=%fused_computation.256 | convolution fusion | flops 301989888 | bytes 2654208 | tf_op jit(solution)/shard_map/dot_general | solution.py:63
  77.3 1.8 %fusion.159 = f32[1024,384]{1,0:T(8,128)} fusion(bf16[1024,384]{1,0:T(8,128)(2,1)S(1)} %bitcast.812, bf16[27,384,384]{2,1,0:T(8,128)(2,1)S(1)} %copy-done.1), kind=kOutput, calls=%fused_computation.260 | convolution fusion | flops 301989888 | bytes 2654208 | tf_op jit(solution)/shard_map/dot_general | solution.py:63
  79.1 1.8 %fusion.161 = f32[1024,384]{1,0:T(8,128)} fusion(bf16[1024,384]{1,0:T(8,128)(2,1)S(1)} %bitcast.811, bf16[27,384,384]{2,1,0:T(8,128)(2,1)S(1)} %copy-done.1), kind=kOutput, calls=%fused_computation.262 | convolution fusion | flops 301989888 | bytes 2654208 | tf_op jit(solution)/shard_map/dot_general | solution.py:63
  80.9 1.8 %fusion.165 = f32[1024,384]{1,0:T(8,128)} fusion(bf16[1024,384]{1,0:T(8,128)(2,1)S(1)} %bitcast.810, bf16[27,384,384]{2,1,0:T(8,128)(2,1)S(1)} %copy-done.1), kind=kOutput, calls=%fused_computation.266 | convolution fusion | flops 301989888 | bytes 2654208 | tf_op jit(solution)/shard_map/dot_general | solution.py:63
  82.7 13.8 %add_add_fusion = f32[1024,384]{1,0:T(8,128)S(1)} fusion(f32[1024,384]{1,0:T(8,128)} %fusion.115, f32[1024,384]{1,0:T(8,128)} %fusion.117, f32[1024,384]{1,0:T(8,128)} %fusion.119, f32[1024,384]{1,0:T(8,128)S(1)} %fusion.121, f32[1024,384]{1,0:T(8,128)} %fusion.123, f32[1024,384]{1,0:T(8,128)} %fusion.125, f32[1024,384]{1,0:T(8,128)} %fusion.127, ...), kind=kOutput, calls=%fused_computation.37 | convolution fusion | flops 312213504 | bytes 43548672 | tf_op jit(solution)/shard_map/dot_general | solution.py:63
  97.1 5.8 %collective-permute-start.3 = (bf16[6,1,2,128]{3,0,2,1:T(8,128)(2,1)S(1)}, bf16[6,1,2,128]{3,0,2,1:T(8,128)(2,1)S(1)}, u32[]{:S(2)}, u32[]{:S(2)}) collective-permute-start(bf16[6,1,2,128]{3,0,2,1:T(8,128)(2,1)S(1)} %get-tuple-element.69), channel_id=1, source_target_pairs={{0,8},{8,16},{16,24},{1,9},{9,17},{17,25},{2,10},{10,18},{18,26},{... | collective-permute-start | bytes 9224 | tf_op jit(solution)/shard_map/ppermute | solution.py:21
  102.8 1.3 collective-permute-start.4
  104.2 1.9 %collective-permute-done.4 = bf16[6,1,2,128]{3,0,2,1:T(8,128)(2,1)S(1)} collective-permute-done((bf16[6,1,2,128]{3,0,2,1:T(8,128)(2,1)S(1)}, bf16[6,1,2,128]{3,0,2,1:T(8,128)(2,1)S(1)}, u32[]{:S(2)}, u32[]{:S(2)}) %collective-permute-start.4) | collective-permute-done | bytes 3104 | tf_op jit(solution)/shard_map/ppermute | solution.py:23
  106.1 4.4 %collective-permute-start.5 = (bf16[6,6,1,128]{3,0,2,1:T(8,128)(2,1)S(1)}, bf16[6,6,1,128]{3,0,2,1:T(8,128)(2,1)S(1)}, u32[]{:S(2)}, u32[]{:S(2)}) collective-permute-start(bf16[6,6,1,128]{3,0,2,1:T(8,128)(2,1)S(1)} %get-tuple-element.67), channel_id=1, source_target_pairs={{0,1},{1,2},{2,3},{3,4},{4,5},{5,6},{6,7},{8,9},{9,10},{10,11},{11... | collective-permute-start | bytes 27656 | tf_op jit(solution)/shard_map/ppermute | solution.py:21
  110.5 1.5 collective-permute-start.6
  112.3 4.2 %collective-permute-done.6 = bf16[6,6,1,128]{3,0,2,1:T(8,128)(2,1)S(1)} collective-permute-done((bf16[6,6,1,128]{3,0,2,1:T(8,128)(2,1)S(1)}, bf16[6,6,1,128]{3,0,2,1:T(8,128)(2,1)S(1)}, u32[]{:S(2)}, u32[]{:S(2)}) %collective-permute-start.6) | collective-permute-done | bytes 9248 | tf_op jit(solution)/shard_map/ppermute | solution.py:23
  129.4 3.1 %collective-permute-start.7 = (bf16[128,1,2,128]{3,0,2,1:T(8,128)(2,1)S(1)}, bf16[128,1,2,128]{3,0,2,1:T(8,128)(2,1)S(1)}, u32[]{:S(2)}, u32[]{:S(2)}) collective-permute-start(bf16[128,1,2,128]{3,0,2,1:T(8,128)(2,1)S(1)} %get-tuple-element.36), channel_id=1, source_target_pairs={{0,8},{8,16},{16,24},{1,9},{9,17},{17,25},{2,10},{10,18},{18,26},{... | collective-permute-start | bytes 196616 | tf_op jit(solution)/shard_map/ppermute | solution.py:21
  132.5 1.3 collective-permute-start.8
  134.3 2.0 %collective-permute-done.8 = bf16[128,1,2,128]{3,0,2,1:T(8,128)(2,1)S(1)} collective-permute-done((bf16[128,1,2,128]{3,0,2,1:T(8,128)(2,1)S(1)}, bf16[128,1,2,128]{3,0,2,1:T(8,128)(2,1)S(1)}, u32[]{:S(2)}, u32[]{:S(2)}) %collective-permute-start.8) | collective-permute-done | bytes 65568 | tf_op jit(solution)/shard_map/ppermute | solution.py:23
  136.4 1.3 collective-permute-start.10
  137.7 5.5 %collective-permute-start.9 = (bf16[128,6,1,128]{3,0,2,1:T(8,128)(2,1)S(1)}, bf16[128,6,1,128]{3,0,2,1:T(8,128)(2,1)S(1)}, u32[]{:S(2)}, u32[]{:S(2)}) collective-permute-start(bf16[128,6,1,128]{3,0,2,1:T(8,128)(2,1)S(1)} %get-tuple-element.34), channel_id=1, source_target_pairs={{0,1},{1,2},{2,3},{3,4},{4,5},{5,6},{6,7},{8,9},{9,10},{10,11},{11... | collective-permute-start | bytes 589832 | tf_op jit(solution)/shard_map/ppermute | solution.py:21
  144.9 6.7 %collective-permute-done.9 = bf16[128,6,1,128]{3,0,2,1:T(8,128)(2,1)S(1)} collective-permute-done((bf16[128,6,1,128]{3,0,2,1:T(8,128)(2,1)S(1)}, bf16[128,6,1,128]{3,0,2,1:T(8,128)(2,1)S(1)}, u32[]{:S(2)}, u32[]{:S(2)}) %collective-permute-start.9) | collective-permute-done | bytes 196640 | tf_op jit(solution)/shard_map/ppermute | solution.py:21
  151.5 1.7 select_maximum_fusion.2
  (149 shorter events, 32.3 us)
Async XLA Ops:
  0.6 96.1 %copy-start = (bf16[384,3]{0,1:T(4,128)(2,1)S(1)}, bf16[384,3]{0,1:T(4,128)(2,1)}, u32[]{:S(2)}) copy-start(bf16[384,3]{0,1:T(4,128)(2,1)} %param.10) | copy-start | bytes 6916
  0.6 5.9 %copy-start.5 = (bf16[27,64,3]{1,0,2:T(8,128)(2,1)S(1)}, bf16[27,64,3]{1,0,2:T(8,128)(2,1)}, u32[]{:S(2)}) copy-start(bf16[27,64,3]{1,0,2:T(8,128)(2,1)} %param.12) | copy-start | bytes 31108
  0.7 6.0 %copy-start.6 = (bf16[3,4,2,128]{3,2,1,0:T(2,128)(2,1)S(1)}, bf16[3,4,2,128]{3,2,1,0:T(2,128)(2,1)}, u32[]{:S(2)}) copy-start(bf16[3,4,2,128]{3,2,1,0:T(2,128)(2,1)} %param.11) | copy-start | bytes 18436
  3.7 10.4 %copy-start.1 = (bf16[27,384,384]{2,1,0:T(8,128)(2,1)S(1)}, bf16[27,384,384]{2,1,0:T(8,128)(2,1)}, u32[]{:S(2)}) copy-start(bf16[27,384,384]{2,1,0:T(8,128)(2,1)} %param.9) | copy-start | bytes 23887876
  3.8 4.5 %collective-permute-start = (bf16[2,2,128,384]{3,2,1,0:T(8,128)(2,1)S(1)}, bf16[2,2,128,384]{3,2,1,0:T(8,128)(2,1)S(1)}, u32[]{:S(2)}, u32[]{:S(2)}) collective-permute-start(bf16[2,2,128,384]{3,2,1,0:T(8,128)(2,1)S(1)} %slice.1161), channel_id=1, source_target_pairs={{0,8},{8,16},{16,24},{1,9},{9,17},{17,25},{2,10},{10,18},{18,26},{... | collective-permute-start | bytes 1179656 | tf_op jit(solution)/shard_map/ppermute | solution.py:10
  8.4 26.9 %collective-permute-start.1 = (bf16[6,1,128,384]{3,2,1,0:T(8,128)(2,1)S(1)}, bf16[6,1,128,384]{3,2,1,0:T(8,128)(2,1)S(1)}, u32[]{:S(2)}, u32[]{:S(2)}) collective-permute-start(bf16[6,1,128,384]{3,2,1,0:T(8,128)(2,1)S(1)} %get-tuple-element.30), channel_id=1, source_target_pairs={{0,1},{1,2},{2,3},{3,4},{4,5},{5,6},{6,7},{8,9},{9,10},{10,11},{11... | collective-permute-start | bytes 1769480 | tf_op jit(solution)/shard_map/ppermute | solution.py:21
  12.7 22.6 %collective-permute-start.2 = (bf16[6,1,128,384]{3,2,1,0:T(8,128)(2,1)S(1)}, bf16[6,1,128,384]{3,2,1,0:T(8,128)(2,1)S(1)}, u32[]{:S(2)}, u32[]{:S(2)}) collective-permute-start(bf16[6,1,128,384]{3,2,1,0:T(8,128)(2,1)S(1)} %get-tuple-element.31), channel_id=1, source_target_pairs={{1,0},{2,1},{3,2},{4,3},{5,4},{6,5},{7,6},{9,8},{10,9},{11,10},{12... | collective-permute-start | bytes 1769480 | tf_op jit(solution)/shard_map/ppermute | solution.py:23
  82.7 13.8 %copy-start.2 = (bf16[4,2,128,384]{3,2,1,0:T(8,128)(2,1)S(1)}, bf16[4,2,128,384]{3,2,1,0:T(8,128)(2,1)}, u32[]{:S(2)}) copy-start(bf16[4,2,128,384]{3,2,1,0:T(8,128)(2,1)} %param.7) | copy-start | bytes 2359300
  96.7 21.4 %copy-start.3 = (bf16[4,2,128,384]{3,2,1,0:T(8,128)(2,1)}, bf16[4,2,128,384]{3,2,1,0:T(8,128)(2,1)S(1)}, u32[]{:S(2)}) copy-start(bf16[4,2,128,384]{3,2,1,0:T(8,128)(2,1)S(1)} %fusion.13) | copy-start | bytes 2359300
  97.1 7.1 %collective-permute-start.3 = (bf16[6,1,2,128]{3,0,2,1:T(8,128)(2,1)S(1)}, bf16[6,1,2,128]{3,0,2,1:T(8,128)(2,1)S(1)}, u32[]{:S(2)}, u32[]{:S(2)}) collective-permute-start(bf16[6,1,2,128]{3,0,2,1:T(8,128)(2,1)S(1)} %get-tuple-element.69), channel_id=1, source_target_pairs={{0,8},{8,16},{16,24},{1,9},{9,17},{17,25},{2,10},{10,18},{18,26},{... | collective-permute-start | bytes 9224 | tf_op jit(solution)/shard_map/ppermute | solution.py:21
  102.8 3.3 %collective-permute-start.4 = (bf16[6,1,2,128]{3,0,2,1:T(8,128)(2,1)S(1)}, bf16[6,1,2,128]{3,0,2,1:T(8,128)(2,1)S(1)}, u32[]{:S(2)}, u32[]{:S(2)}) collective-permute-start(bf16[6,1,2,128]{3,0,2,1:T(8,128)(2,1)S(1)} %get-tuple-element.70), channel_id=1, source_target_pairs={{8,0},{16,8},{24,16},{9,1},{17,9},{25,17},{10,2},{18,10},{26,18},{... | collective-permute-start | bytes 9224 | tf_op jit(solution)/shard_map/ppermute | solution.py:23
  106.1 6.1 %collective-permute-start.5 = (bf16[6,6,1,128]{3,0,2,1:T(8,128)(2,1)S(1)}, bf16[6,6,1,128]{3,0,2,1:T(8,128)(2,1)S(1)}, u32[]{:S(2)}, u32[]{:S(2)}) collective-permute-start(bf16[6,6,1,128]{3,0,2,1:T(8,128)(2,1)S(1)} %get-tuple-element.67), channel_id=1, source_target_pairs={{0,1},{1,2},{2,3},{3,4},{4,5},{5,6},{6,7},{8,9},{9,10},{10,11},{11... | collective-permute-start | bytes 27656 | tf_op jit(solution)/shard_map/ppermute | solution.py:21
  110.5 6.0 %collective-permute-start.6 = (bf16[6,6,1,128]{3,0,2,1:T(8,128)(2,1)S(1)}, bf16[6,6,1,128]{3,0,2,1:T(8,128)(2,1)S(1)}, u32[]{:S(2)}, u32[]{:S(2)}) collective-permute-start(bf16[6,6,1,128]{3,0,2,1:T(8,128)(2,1)S(1)} %get-tuple-element.68), channel_id=1, source_target_pairs={{1,0},{2,1},{3,2},{4,3},{5,4},{6,5},{7,6},{9,8},{10,9},{11,10},{12... | collective-permute-start | bytes 27656 | tf_op jit(solution)/shard_map/ppermute | solution.py:23
  128.6 5.1 %copy-start.4 = (bf16[27,128,64]{1,2,0:T(8,128)(2,1)S(1)}, bf16[27,128,64]{1,2,0:T(8,128)(2,1)}, u32[]{:S(2)}) copy-start(bf16[27,128,64]{1,2,0:T(8,128)(2,1)} %param.13) | copy-start | bytes 1327108
  129.4 5.0 %collective-permute-start.7 = (bf16[128,1,2,128]{3,0,2,1:T(8,128)(2,1)S(1)}, bf16[128,1,2,128]{3,0,2,1:T(8,128)(2,1)S(1)}, u32[]{:S(2)}, u32[]{:S(2)}) collective-permute-start(bf16[128,1,2,128]{3,0,2,1:T(8,128)(2,1)S(1)} %get-tuple-element.36), channel_id=1, source_target_pairs={{0,8},{8,16},{16,24},{1,9},{9,17},{17,25},{2,10},{10,18},{18,26},{... | collective-permute-start | bytes 196616 | tf_op jit(solution)/shard_map/ppermute | solution.py:21
  132.5 3.8 %collective-permute-start.8 = (bf16[128,1,2,128]{3,0,2,1:T(8,128)(2,1)S(1)}, bf16[128,1,2,128]{3,0,2,1:T(8,128)(2,1)S(1)}, u32[]{:S(2)}, u32[]{:S(2)}) collective-permute-start(bf16[128,1,2,128]{3,0,2,1:T(8,128)(2,1)S(1)} %get-tuple-element.37), channel_id=1, source_target_pairs={{8,0},{16,8},{24,16},{9,1},{17,9},{25,17},{10,2},{18,10},{26,18},{... | collective-permute-start | bytes 196616 | tf_op jit(solution)/shard_map/ppermute | solution.py:23
  136.4 8.5 %collective-permute-start.10 = (bf16[128,6,1,128]{3,0,2,1:T(8,128)(2,1)S(1)}, bf16[128,6,1,128]{3,0,2,1:T(8,128)(2,1)S(1)}, u32[]{:S(2)}, u32[]{:S(2)}) collective-permute-start(bf16[128,6,1,128]{3,0,2,1:T(8,128)(2,1)S(1)} %get-tuple-element.35), channel_id=1, source_target_pairs={{1,0},{2,1},{3,2},{4,3},{5,4},{6,5},{7,6},{9,8},{10,9},{11,10},{12... | collective-permute-start | bytes 589832 | tf_op jit(solution)/shard_map/ppermute | solution.py:23
  137.7 13.8 %collective-permute-start.9 = (bf16[128,6,1,128]{3,0,2,1:T(8,128)(2,1)S(1)}, bf16[128,6,1,128]{3,0,2,1:T(8,128)(2,1)S(1)}, u32[]{:S(2)}, u32[]{:S(2)}) collective-permute-start(bf16[128,6,1,128]{3,0,2,1:T(8,128)(2,1)S(1)} %get-tuple-element.34), channel_id=1, source_target_pairs={{0,1},{1,2},{2,3},{3,4},{4,5},{5,6},{6,7},{8,9},{9,10},{10,11},{11... | collective-permute-start | bytes 589832 | tf_op jit(solution)/shard_map/ppermute | solution.py:21
where the time goes:
time: 169 us
  matrix products  89 us (53%)
  waiting for transfers between devices  32.9 us (19%)
  starting transfers between devices  32.5 us (19%)
  other arithmetic  8.19 us (5%)
  local copies, waits for them, and re-layouts  4.29 us (3%)
  between operations  1.84 us (1%)
    dot_general x27, matrix products, per_device(): jnp.dot(piece, conv_weight[tap], preferred_element_type=jnp.float32)  60.3 us
    dot_general x108, matrix products, conv_valid(): jnp.einsum('oc,cthw->othw', weights[tap], piece, preferred_element_type=j...  28.4 us
    ppermute x5, waiting for transfers between devices, extended_2(): lax.ppermute(tail, axis, [(i, (i + 1) % count) for i in range(ends)])  24.2 us
    ppermute x5, starting transfers between devices, extended_2(): lax.ppermute(tail, axis, [(i, (i + 1) % count) for i in range(ends)])  23 us
    ppermute x5, waiting for transfers between devices, extended_2(): lax.ppermute(head, axis, [((i + 1) % count, i) for i in range(ends)])  8.78 us
    ppermute x5, starting transfers between devices, extended_2(): lax.ppermute(head, axis, [((i + 1) % count, i) for i in range(ends)])  6.68 us
    slice x2, local copies, waits for them, and re-layouts, per_device(): extended[dt:dt + frames, dh:dh + height, dw:dw + width].reshape(-1, chans)  4.12 us
    concatenate x8, other arithmetic, extended_2(): jnp.concatenate([lax.ppermute(tail, axis, [(i, (i + 1) % count) for i in...  4 us
  transfers between devices with their start and end apart: 11, of which 6 were waited for; matrix products, arithmetic and copies ran while one was open for 4% of the time, Pallas kernels for 0%

commit v1 on v0

v1 whole, which is shorter than its diff:
```python
import functools

import jax
import jax.numpy as jnp
from jax import lax
from jax.experimental import pallas as pl
from jax.experimental.pallas import tpu as pltpu
from jax.sharding import PartitionSpec as P

MESH = pl.DeviceIdType.MESH
F32 = jnp.float32
BF16 = jnp.bfloat16
SIDES = [(i, j) for i in (-1, 0, 1) for j in (-1, 0, 1) if (i, j) != (0, 0)]


def leaky(value):
    return jnp.maximum(value, 0.2 * value)


def span(step, size):
    if step == 0:
        return 2, 2, size
    return (size, 0, 2) if step > 0 else (2, size + 2, 2)


def shifted(value, step):
    width = value.shape[-1]
    lane = lax.broadcasted_iota(jnp.int32, value.shape, value.ndim - 1)
    moved = pltpu.roll(value, step % width, value.ndim - 1)
    edge = 0 if step > 0 else width - 1
    return jnp.where(lane == edge, 0.0, moved)


def tripled(value):
    row = lax.broadcasted_iota(jnp.int32, value.shape, 0)
    out = jnp.where(row < 3, shifted(value, 1), jnp.where(row < 6, value, shifted(value, -1)))
    return jnp.where(row < 9, out, 0.0).astype(BF16)


def kernel(
    slabs, bands, lat, gain, w_hbm, rgb, real, d1, d2, dec, match,
    wv, ext, acc, grid, feat, second, w1, w2, real32,
    w_sem, row_s, row_r, tm_s, tm_r, relay_s, relay_r, g_s, g_r,
):
    frames, height, width, chans = lat.shape
    depth, depth2 = d1.shape[1], d2.shape[1]
    tm, band = lax.axis_index("tm"), lax.axis_index("rows")

    def exists(i, j):
        ok = jnp.bool_(True)
        if i:
            ok = ok & (tm + i >= 0) & (tm + i < slabs)
        if j:
            ok = ok & (band + j >= 0) & (band + j < bands)
        return ok

    loads = []
    for dh in range(3):
        for dw in range(3):
            copy = pltpu.make_async_copy(
                w_hbm.at[:, dh, dw], wv.at[dh, :, :, pl.ds(dw * chans, chans)], w_sem.at[dh, dw]
            )
            copy.start()
            loads.append(copy)

    barrier = pltpu.get_barrier_semaphore()
    count = jnp.int32(0)
    for i, j in SIDES:
        ok = exists(i, j)
        count = count + ok.astype(jnp.int32)

        @pl.when(ok)
        def _(i=i, j=j):
            pl.semaphore_signal(barrier, inc=1, device_id=(tm + i, band + j), device_id_type=MESH)

    for f in range(frames):
        for r in range(height):
            x = lat[f, r].astype(F32)
            scale = lax.rsqrt(jnp.mean(x * x, axis=-1, keepdims=True) + 1e-06)
            ext[f + 2, r + 1] = jax.nn.silu(x * scale * gain[...]).astype(BF16)

    @pl.when(tm == 0)
    def _():
        ext[0:2] = jnp.zeros((2,) + ext.shape[1:], BF16)

    @pl.when((band == 0) & (tm > 0))
    def _():
        ext[0:2, 0] = jnp.zeros((2, width, chans), BF16)

    @pl.when((band == bands - 1) & (tm > 0))
    def _():
        ext[0:2, height + 1] = jnp.zeros((2, width, chans), BF16)

    @pl.when(band == 0)
    def _():
        ext[2:, 0] = jnp.zeros((frames, width, chans), BF16)

    @pl.when(band == bands - 1)
    def _():
        ext[2:, height + 1] = jnp.zeros((frames, width, chans), BF16)

    pl.semaphore_wait(barrier, count)

    halves = [(frames, 2), (2, frames - 2)]

    def row_copy(side, half):
        start, size = halves[half]
        mine, theirs = (1, height + 1) if side < 0 else (height, 0)
        where = 0 if side < 0 else 1
        return pltpu.make_async_remote_copy(
            src_ref=ext.at[pl.ds(start, size), mine],
            dst_ref=ext.at[pl.ds(start, size), theirs],
            send_sem=row_s.at[where, half],
            recv_sem=row_r.at[where, half],
            device_id=(tm, band + side),
            device_id_type=MESH,
        )

    tm_copy = pltpu.make_async_remote_copy(
        src_ref=ext.at[pl.ds(frames, 2), pl.ds(1, height)],
        dst_ref=ext.at[pl.ds(0, 2), pl.ds(1, height)],
        send_sem=tm_s,
        recv_sem=tm_r,
        device_id=(tm + 1, band),
        device_id_type=MESH,
    )

    def relay_copy(where):
        row = 0 if where else height + 1
        return pltpu.make_async_remote_copy(
            src_ref=ext.at[pl.ds(frames, 2), row],
            dst_ref=ext.at[pl.ds(0, 2), row],
            send_sem=relay_s.at[where],
            recv_sem=relay_r.at[where],
            device_id=(tm + 1, band),
            device_id_type=MESH,
        )

    def grid_copy(kind, side):
        i, j = SIDES[side]
        (fs, fd, fn), (rs, rd, rn) = span(i, frames), span(j, height)
        return pltpu.make_async_remote_copy(
            src_ref=grid.at[kind, pl.ds(fs, fn), pl.ds(rs, rn)],
            dst_ref=grid.at[kind, pl.ds(fd, fn), pl.ds(rd, rn)],
            send_sem=g_s.at[kind, side],
            recv_sem=g_r.at[kind, side],
            device_id=(tm + i, band + j),
            device_id_type=MESH,
        )

    def when(ok, action):
        pl.when(ok)(action)

    when(exists(1, 0), lambda: tm_copy.start())
    for half in (0, 1):
        for side in (-1, 1):
            when(exists(0, side), lambda: row_copy(side, half).start())

    def grid_zero(kind):
        for side in range(len(SIDES)):
            i, j = SIDES[side]
            (_, fd, fn), (_, rd, rn) = span(i, frames), span(j, height)

            @pl.when(jnp.logical_not(exists(-i, -j)))
            def _():
                grid[kind, fd:fd + fn, rd:rd + rn] = jnp.zeros((fn, rn, 16, width), BF16)

    def grid_send(kind):
        for side in range(len(SIDES)):
            when(exists(*SIDES[side]), lambda: grid_copy(kind, side).start())

    def grid_wait(kind):
        for side in range(len(SIDES)):
            i, j = SIDES[side]
            when(exists(-i, -j), lambda: grid_copy(kind, side).wait_recv())

    grid_zero(0)
    grid_zero(1)
    real32[...] = real[...].astype(F32)
    row = lax.broadcasted_iota(jnp.int32, (16, width), 0)
    for f in range(frames):
        for r in range(height):
            b0, b1, b2 = [
                jnp.broadcast_to(real32[c, f, r:r + 1], (16, width)) for c in range(3)
            ]
            cell = jnp.where(row % 3 == 0, b0, jnp.where(row % 3 == 1, b1, b2))
            grid[1, f + 2, r + 2] = tripled(cell)
    grid_send(1)

    def lhs(f0, nf, row):
        return jnp.concatenate(
            [ext[f0 + dt:f0 + dt + nf, row].reshape(nf * width, chans) for dt in range(3)], axis=1
        )

    def own(f0, nf):
        for r in range(height):
            taps = [dh for dh in range(3) if 1 <= r + dh <= height]
            left = jnp.concatenate([lhs(f0, nf, r + dh) for dh in taps], axis=1)
            right = wv[taps[0]:taps[-1] + 1].reshape(len(taps) * 3 * chans, 3 * chans)
            total = jnp.dot(left, right, preferred_element_type=F32)
            acc[r, f0:f0 + nf] = total.reshape(nf, width, 3 * chans)

    for copy in loads:
        copy.wait()
    own(frames - 2, 2)
    when(exists(-1, 0), lambda: tm_copy.wait_recv())
    own(0, frames - 2)

    for where, side in ((0, -1), (1, 1)):
        when(exists(0, -side), lambda: row_copy(side, 0).wait_recv())
        when(exists(0, -side) & exists(1, 0), lambda: relay_copy(where).start())

    reach = 9 * 16
    r3 = lax.broadcasted_iota(jnp.int32, (3, reach), 0)
    c3 = lax.broadcasted_iota(jnp.int32, (3, reach), 1) % 16
    pick = jnp.where((c3 < 9) & (c3 % 3 == r3), 1.0, 0.0).astype(BF16)
    col = lax.broadcasted_iota(jnp.int32, (depth, reach), 1)
    spread = jnp.zeros((depth, reach), F32)
    for tap in range(27):
        part = jnp.dot(d1[tap], pick, preferred_element_type=F32)
        spread = jnp.where((col // 16 == tap // 3) & (col % 16 // 3 == tap % 3), part, spread)
    w1[...] = spread.astype(BF16)
    for tap in range(27):
        k, dw = tap // 3, tap % 3
        w2[dw * depth2:(dw + 1) * depth2, k * depth:(k + 1) * depth] = d2[tap]
    r16 = lax.broadcasted_iota(jnp.int32, (16, 3), 0)
    c16 = lax.broadcasted_iota(jnp.int32, (16, 3), 1)
    pick16 = jnp.where((r16 < 9) & (r16 % 3 == c16), 1.0, 0.0).astype(BF16)
    rgb16 = lax.dot_general(
        pick16, rgb[...], (((1,), (1,)), ((), ())), preferred_element_type=F32
    ).astype(BF16)

    def first_layer(kind):
        for t in range(frames + 2):
            cells = [
                jnp.concatenate(
                    [grid[kind, t + dt, r:r + 3].reshape(48, width) for dt in range(3)], axis=0
                )
                for r in range(height + 2)
            ]
            out = leaky(
                jnp.dot(w1[...], jnp.concatenate(cells, axis=1), preferred_element_type=F32)
            )
            for r in range(height + 2):
                value = out[:, r * width:(r + 1) * width]
                when_t, when_r = tm * frames + t - 1, band * height + r - 1
                inside = (
                    (when_t >= 0) & (when_t < slabs * frames)
                    & (when_r >= 0) & (when_r < bands * height)
                )
                feat[kind, t, r] = jnp.where(inside, value, 0.0).astype(BF16)

    def second_layer(kind, t):
        cells = [
            jnp.concatenate(
                [feat[kind, t + dt, r:r + 3].reshape(3 * depth, width) for dt in range(3)], axis=0
            )
            for r in range(height)
        ]
        out = jnp.dot(w2[...], jnp.concatenate(cells, axis=1), preferred_element_type=F32)
        result = []
        for r in range(height):
            part = out[:, r * width:(r + 1) * width]
            total = (
                shifted(part[:depth2], 1)
                + part[depth2:2 * depth2]
                + shifted(part[2 * depth2:], -1)
            )
            result.append(leaky(total).astype(BF16))
        return result

    grid_wait(1)
    first_layer(1)
    for t in range(frames):
        for r, value in enumerate(second_layer(1, t)):
            second[t, r] = value

    for where, side in ((0, -1), (1, 1)):
        when(exists(0, -side), lambda: row_copy(side, 1).wait_recv())
        when(exists(0, -side) & exists(-1, 0), lambda: relay_copy(where).wait_recv())
    for r, dh, row_in in ((0, 0, 0), (height - 1, 2, height + 1)):
        total = jnp.dot(
            lhs(0, frames, row_in),
            wv[dh].reshape(3 * chans, 3 * chans),
            preferred_element_type=F32,
        )
        acc[r] = acc[r] + total.reshape(frames, width, 3 * chans)

    line = lax.broadcasted_iota(jnp.int32, (width, chans), 0)
    for r in range(height):
        for f in range(frames):
            before = pltpu.roll(acc[r, f, :, 0:chans], 1, 0)
            after = pltpu.roll(acc[r, f, :, 2 * chans:3 * chans], width - 1, 0)
            conv = (
                jnp.where(line == 0, 0.0, before)
                + acc[r, f, :, chans:2 * chans]
                + jnp.where(line == width - 1, 0.0, after)
            )
            value = (lat[f, r].astype(F32) + conv).astype(BF16)
            dec[f, r] = value
            colour = lax.dot_general(
                rgb16, value, (((1,), (1,)), ((), ())), preferred_element_type=F32
            )
            grid[0, f + 2, r + 2] = tripled(colour.astype(BF16).astype(F32))
    grid_send(0)
    grid_wait(0)
    first_layer(0)
    for t in range(frames):
        for r, value in enumerate(second_layer(0, t)):
            near = jnp.abs(feat[0, t + 1, r + 1].astype(F32) - feat[1, t + 1, r + 1].astype(F32))
            far = jnp.abs(value.astype(F32) - second[t, r].astype(F32))
            match[t, r:r + 1] = (
                jnp.sum(near, axis=0, keepdims=True) / depth
                + jnp.sum(far, axis=0, keepdims=True) / depth2
            )

    when(exists(1, 0), lambda: tm_copy.wait_send())
    for where, side in ((0, -1), (1, 1)):
        for half in (0, 1):
            when(exists(0, side), lambda: row_copy(side, half).wait_send())
        when(exists(0, -side) & exists(1, 0), lambda: relay_copy(where).wait_send())
    for kind in (0, 1):
        for side in range(len(SIDES)):
            when(exists(*SIDES[side]), lambda: grid_copy(kind, side).wait_send())


def per_device(
    slabs, bands, latent_feat, norm_gain, conv_weight, rgb_weight, real_frames, disc_first, disc_second
):
    frames, height, width, chans = latent_feat.shape
    depth, depth2 = disc_first.shape[1], disc_second.shape[1]
    vmem = pl.BlockSpec(memory_space=pltpu.VMEM)
    dma = pltpu.SemaphoreType.DMA
    return pl.pallas_call(
        functools.partial(kernel, slabs, bands),
        out_shape=(
            jax.ShapeDtypeStruct(latent_feat.shape, BF16),
            jax.ShapeDtypeStruct((frames, height, width), F32),
        ),
        in_specs=[vmem, vmem, pl.BlockSpec(memory_space=pl.ANY), vmem, vmem, vmem, vmem],
        out_specs=(vmem, vmem),
        scratch_shapes=[
            pltpu.VMEM((3, 3, chans, 3 * chans), BF16),
            pltpu.VMEM((frames + 2, height + 2, width, chans), BF16),
            pltpu.VMEM((height, frames, width, 3 * chans), F32),
            pltpu.VMEM((2, frames + 4, height + 4, 16, width), BF16),
            pltpu.VMEM((2, frames + 2, height + 2, depth, width), BF16),
            pltpu.VMEM((frames, height, depth2, width), BF16),
            pltpu.VMEM((depth, 9 * 16), BF16),
            pltpu.VMEM((3 * depth2, 9 * depth), BF16),
            pltpu.VMEM(real_frames.shape, F32),
            dma((3, 3)),
            dma((2, 2)),
            dma((2, 2)),
            dma,
            dma,
            dma((2,)),
            dma((2,)),
            dma((2, 8)),
            dma((2, 8)),
        ],
        compiler_params=pltpu.CompilerParams(
            collective_id=0, has_side_effects=True, vmem_limit_bytes=48 * 1024 * 1024
        ),
    )(
        latent_feat,
        norm_gain.reshape(1, chans),
        conv_weight.reshape(3, 3, 3, chans, chans),
        rgb_weight,
        real_frames,
        disc_first,
        disc_second,
    )


def solution(mesh):
    placed = (P("tm", "rows", None, None), P(), P(), P(), P(None, "tm", "rows", None), P(), P())
    return jax.shard_map(
        functools.partial(per_device, mesh.shape["tm"], mesh.shape["rows"]),
        mesh=mesh,
        in_specs=placed,
        out_specs=(P("tm", "rows", None, None), P("tm", "rows", None)),
        check_vma=False,
    )
```

time: 169 us -> 42.7 us (0.25)
  matrix products: 89 us -> 0 us
  Pallas kernels: 0 us -> 34.3 us
  waiting for transfers between devices: 32.9 us -> 0 us
  starting transfers between devices: 32.5 us -> 0 us
  other arithmetic: 8.19 us -> 0 us
  local copies, waits for them, and re-layouts: 4.29 us -> 7.33 us
    dot_general x136 -> x0, matrix products: 89 us -> none  [the longest x27 60.3 us: per_device(): jnp.dot(piece, conv_weight[tap], preferred_element_type=jnp.float32)]
    pallas_call x0 -> x1, Pallas kernels: none -> 34.3 us  [per_device(): pl.pallas_call(functools.partial(kernel, slabs, bands), out_shape=(jax.Sh...]
    ppermute x11 -> x0, waiting for transfers between devices: 32.9 us -> none  [the longest x5 24.2 us: extended_2(): lax.ppermute(tail, axis, [(i, (i + 1) % count) for i in range(ends)])]
    ppermute x11 -> x0, starting transfers between devices: 32.5 us -> none  [the longest x5 23 us: extended_2(): lax.ppermute(tail, axis, [(i, (i + 1) % count) for i in range(ends)])]
    unnamed x15 -> x9, local copies, waits for them, and re-layouts: 0.05 us -> 6.64 us
    concatenate x10 -> x0, other arithmetic: 4.31 us -> none  [the longest x8 4 us: extended_2(): jnp.concatenate([lax.ppermute(tail, axis, [(i, (i + 1) % count) for i in...]
    slice x7 -> x0, local copies, waits for them, and re-layouts: 4.24 us -> none  [the longest x2 4.12 us: per_device(): extended[dt:dt + frames, dh:dh + height, dw:dw + width].reshape(-1, chans)]
    convert_element_type x2 -> x0, other arithmetic: 1.86 us -> none  [the longest x1 1.66 us: per_device(): act = jax.nn.silu(normed).astype(jnp.bfloat16)]
  transfers between devices with their start and end apart: 11 -> 0, of which waited for: 6 -> 0; matrix products, arithmetic and copies ran while one was open for 4% -> 0% of each run, Pallas kernels for 0% -> 0%
where the time goes in v1:
time: 42.7 us; the launch traced here: 42.3 us
  Pallas kernels  34.3 us (80%)
  local copies, waits for them, and re-layouts  7.33 us (17%)
  between operations  0.65 us (2%)
    pallas_call x1, Pallas kernels, per_device(): pl.pallas_call(functools.partial(kernel, slabs, bands), out_shape=(jax.Sh...  34.3 us
    unnamed x9, local copies, waits for them, and re-layouts  6.64 us

profile of v1, /device:TPU:0, one launch (start us, length us, event | category | flops | bytes accessed | tf_op | source)
XLA Modules:
  0.0 42.3 jit_solution(17927312077117894807)
XLA Ops:
  0.6 0.7 %reshape.10.gain = f32[1,384]{1,0:T(1,128)S(1)} reshape(f32[384]{0:T(512)} %param.8) | data formatting | bytes 3072 | tf_op jit(solution)/shard_map/reshape | solution.py:367
  1.3 0.9 %copy.9.rgb = bf16[384,3]{1,0:T(8,128)(2,1)S(1)} copy(bf16[384,3]{0,1:T(4,128)(2,1)} %param.10) | data formatting | bytes 4608 | tf_op args[3]
  2.2 1.1 %copy.10.d1 = bf16[27,64,3]{2,1,0:T(8,128)(2,1)S(1)} copy(bf16[27,64,3]{1,0,2:T(8,128)(2,1)} %param.12) | data formatting | bytes 20736 | tf_op args[5]
  3.2 1.4 %copy.11.d2 = bf16[27,128,64]{2,1,0:T(8,128)(2,1)S(1)} copy(bf16[27,128,64]{1,2,0:T(8,128)(2,1)} %param.13) | data formatting | bytes 884736 | tf_op args[6]
  4.7 0.0 copy-start
  4.7 1.1 %copy-done = bf16[4,2,128,384]{3,2,1,0:T(8,128)(2,1)S(1)} copy-done((bf16[4,2,128,384]{3,2,1,0:T(8,128)(2,1)S(1)}, bf16[4,2,128,384]{3,2,1,0:T(8,128)(2,1)}, u32[]{:S(2)}) %copy-start) | copy-done | bytes 786456
  5.8 0.0 copy-start.1
  5.8 0.7 %copy-done.1 = bf16[3,4,2,128]{3,2,1,0:T(2,128)(2,1)S(1)} copy-done((bf16[3,4,2,128]{3,2,1,0:T(2,128)(2,1)S(1)}, bf16[3,4,2,128]{3,2,1,0:T(2,128)(2,1)}, u32[]{:S(2)}) %copy-start.1) | copy-done | bytes 6168
  6.5 34.3 %shard_map.86 = (bf16[4,2,128,384]{3,2,1,0:T(8,128)(2,1)S(1)}, f32[4,2,128]{2,1,0:T(2,128)S(1)}) custom-call(bf16[4,2,128,384]{3,2,1,0:T(8,128)(2,1)S(1)} %copy-done, f32[1,384]{1,0:T(1,128)S(1)} %reshape.10.gain, bf16[3,3,3,384,384]{4,3,2,1,0:T(8,128)(2,1)} %bitcast.1, bf16[384,3]{1,0:T(8,128)(2,1)S(1)} %copy.9.rgb, bf16[3,4,2,128]{3,2,1,0:T(2,128)(2,1)S(1)} %copy-done.1, ...), custom_call_target="tpu_custom_call" | custom-call | tf_op jit(solution)/shard_map/pallas_call | solution.py:334
  40.8 0.9 %copy.14 = bf16[4,2,128,384]{3,2,1,0:T(8,128)(2,1)} copy(bf16[4,2,128,384]{3,2,1,0:T(8,128)(2,1)S(1)} %get-tuple-element.4) | data formatting | bytes 1572864
  41.7 0.6 %copy.15 = f32[4,2,128]{2,1,0:T(2,128)} copy(f32[4,2,128]{2,1,0:T(2,128)S(1)} %get-tuple-element.5) | data formatting | bytes 8192
Async XLA Ops:
  4.7 1.1 %copy-start = (bf16[4,2,128,384]{3,2,1,0:T(8,128)(2,1)S(1)}, bf16[4,2,128,384]{3,2,1,0:T(8,128)(2,1)}, u32[]{:S(2)}) copy-start(bf16[4,2,128,384]{3,2,1,0:T(8,128)(2,1)} %lat.1) | copy-start | bytes 2359300
  5.8 0.7 %copy-start.1 = (bf16[3,4,2,128]{3,2,1,0:T(2,128)(2,1)S(1)}, bf16[3,4,2,128]{3,2,1,0:T(2,128)(2,1)}, u32[]{:S(2)}) copy-start(bf16[3,4,2,128]{3,2,1,0:T(2,128)(2,1)} %real.1) | copy-start | bytes 18436

commit v2 on v1

--- a/solution.py
+++ b/solution.py
@@ -38,12 +38,13 @@
 
 
 def kernel(
-    slabs, bands, lat, gain, w_hbm, rgb, real, d1, d2, dec, match,
+    slabs, bands, lat_in, gain_in, w_hbm, rgb_in, real_in, d1_in, d2_in, dec, match,
+    lat, gain, rgb, real, d1, d2,
     wv, ext, acc, grid, feat, second, w1, w2, real32,
-    w_sem, row_s, row_r, tm_s, tm_r, relay_s, relay_r, g_s, g_r,
+    in_sem, d2_sem, w_sem, row_s, row_r, tm_s, tm_r, relay_s, relay_r, g_s, g_r,
 ):
     frames, height, width, chans = lat.shape
-    depth, depth2 = d1.shape[1], d2.shape[1]
+    depth, depth2 = d1.shape[2], d2.shape[1] // 3
     tm, band = lax.axis_index("tm"), lax.axis_index("rows")
 
     def exists(i, j):
@@ -54,6 +55,29 @@
             ok = ok & (band + j >= 0) & (band + j < bands)
         return ok
 
+    barrier = pltpu.get_barrier_semaphore()
+    count = jnp.int32(0)
+    for i, j in SIDES:
+        ok = exists(i, j)
+        count = count + ok.astype(jnp.int32)
+
+        @pl.when(ok)
+        def _(i=i, j=j):
+            pl.semaphore_signal(barrier, inc=1, device_id=(tm + i, band + j), device_id_type=MESH)
+
+    inputs = [(lat_in, lat), (gain_in, gain), (real_in, real), (rgb_in, rgb), (d1_in, d1)]
+    inputs = [pltpu.make_async_copy(a, b, in_sem.at[i]) for i, (a, b) in enumerate(inputs)]
+    for dw in range(3):
+        for k in range(9):
+            inputs.append(
+                pltpu.make_async_copy(
+                    d2_in.at[k, dw],
+                    d2.at[pl.ds(k * depth, depth), pl.ds(dw * depth2, depth2)],
+                    d2_sem.at[k, dw],
+                )
+            )
+    for copy in inputs[:2]:
+        copy.start()
     loads = []
     for dh in range(3):
         for dw in range(3):
@@ -62,22 +86,17 @@
             )
             copy.start()
             loads.append(copy)
-
-    barrier = pltpu.get_barrier_semaphore()
-    count = jnp.int32(0)
-    for i, j in SIDES:
-        ok = exists(i, j)
-        count = count + ok.astype(jnp.int32)
-
-        @pl.when(ok)
-        def _(i=i, j=j):
-            pl.semaphore_signal(barrier, inc=1, device_id=(tm + i, band + j), device_id_type=MESH)
-
+    for copy in inputs[2:]:
+        copy.start()
+
+    inputs[0].wait()
+    inputs[1].wait()
+    gains = gain[...].reshape(1, chans)
     for f in range(frames):
         for r in range(height):
             x = lat[f, r].astype(F32)
             scale = lax.rsqrt(jnp.mean(x * x, axis=-1, keepdims=True) + 1e-06)
-            ext[f + 2, r + 1] = jax.nn.silu(x * scale * gain[...]).astype(BF16)
+            ext[f + 2, r + 1] = jax.nn.silu(x * scale * gains).astype(BF16)
 
     @pl.when(tm == 0)
     def _():
@@ -176,6 +195,7 @@
 
     grid_zero(0)
     grid_zero(1)
+    inputs[2].wait()
     real32[...] = real[...].astype(F32)
     row = lax.broadcasted_iota(jnp.int32, (16, width), 0)
     for f in range(frames):
@@ -210,25 +230,26 @@
         when(exists(0, -side), lambda: row_copy(side, 0).wait_recv())
         when(exists(0, -side) & exists(1, 0), lambda: relay_copy(where).start())
 
+    for copy in inputs[3:]:
+        copy.wait()
     reach = 9 * 16
-    r3 = lax.broadcasted_iota(jnp.int32, (3, reach), 0)
-    c3 = lax.broadcasted_iota(jnp.int32, (3, reach), 1) % 16
-    pick = jnp.where((c3 < 9) & (c3 % 3 == r3), 1.0, 0.0).astype(BF16)
-    col = lax.broadcasted_iota(jnp.int32, (depth, reach), 1)
+    tap = lax.broadcasted_iota(jnp.int32, (27, reach), 0)
+    col = lax.broadcasted_iota(jnp.int32, (27, reach), 1)
     spread = jnp.zeros((depth, reach), F32)
-    for tap in range(27):
-        part = jnp.dot(d1[tap], pick, preferred_element_type=F32)
-        spread = jnp.where((col // 16 == tap // 3) & (col % 16 // 3 == tap % 3), part, spread)
+    for c in range(3):
+        pick = (col // 16 == tap // 3) & (col % 16 == tap % 3 * 3 + c)
+        spread = spread + lax.dot_general(
+            d1[c],
+            jnp.where(pick, 1.0, 0.0).astype(BF16),
+            (((0,), (0,)), ((), ())),
+            preferred_element_type=F32,
+        )
     w1[...] = spread.astype(BF16)
-    for tap in range(27):
-        k, dw = tap // 3, tap % 3
-        w2[dw * depth2:(dw + 1) * depth2, k * depth:(k + 1) * depth] = d2[tap]
+    w2[...] = d2[...].T
     r16 = lax.broadcasted_iota(jnp.int32, (16, 3), 0)
     c16 = lax.broadcasted_iota(jnp.int32, (16, 3), 1)
     pick16 = jnp.where((r16 < 9) & (r16 % 3 == c16), 1.0, 0.0).astype(BF16)
-    rgb16 = lax.dot_general(
-        pick16, rgb[...], (((1,), (1,)), ((), ())), preferred_element_type=F32
-    ).astype(BF16)
+    rgb16 = jnp.dot(pick16, rgb[...], preferred_element_type=F32).astype(BF16)
 
     def first_layer(kind):
         for t in range(frames + 2):
@@ -260,11 +281,11 @@
         out = jnp.dot(w2[...], jnp.concatenate(cells, axis=1), preferred_element_type=F32)
         result = []
         for r in range(height):
-            part = out[:, r * width:(r + 1) * width]
+            taps = out[:, r * width:(r + 1) * width]
             total = (
-                shifted(part[:depth2], 1)
-                + part[depth2:2 * depth2]
-                + shifted(part[2 * depth2:], -1)
+                shifted(taps[:depth2], 1)
+                + taps[depth2:2 * depth2]
+                + shifted(taps[2 * depth2:], -1)
             )
             result.append(leaky(total).astype(BF16))
         return result
@@ -275,16 +296,22 @@
         for r, value in enumerate(second_layer(1, t)):
             second[t, r] = value
 
+    def halo(early):
+        for r, dh, row_in in ((0, 0, 0), (height - 1, 2, height + 1)):
+            for dt in range(3):
+                pairs = [(t, t + dt) for t in range(frames)]
+                pairs = [(t, f) for t, f in pairs if (2 <= f < frames) != early]
+                left = jnp.concatenate([ext[f, row_in] for _, f in pairs], axis=0)
+                total = jnp.dot(left, wv[dh, dt], preferred_element_type=F32)
+                for n, (t, _) in enumerate(pairs):
+                    acc[r, t] = acc[r, t] + total[n * width:(n + 1) * width]
+
+    for where, side in ((0, -1), (1, 1)):
+        when(exists(0, -side) & exists(-1, 0), lambda: relay_copy(where).wait_recv())
+    halo(True)
     for where, side in ((0, -1), (1, 1)):
         when(exists(0, -side), lambda: row_copy(side, 1).wait_recv())
-        when(exists(0, -side) & exists(-1, 0), lambda: relay_copy(where).wait_recv())
-    for r, dh, row_in in ((0, 0, 0), (height - 1, 2, height + 1)):
-        total = jnp.dot(
-            lhs(0, frames, row_in),
-            wv[dh].reshape(3 * chans, 3 * chans),
-            preferred_element_type=F32,
-        )
-        acc[r] = acc[r] + total.reshape(frames, width, 3 * chans)
+    halo(False)
 
     line = lax.broadcasted_iota(jnp.int32, (width, chans), 0)
     for r in range(height):
@@ -337,9 +364,15 @@
             jax.ShapeDtypeStruct(latent_feat.shape, BF16),
             jax.ShapeDtypeStruct((frames, height, width), F32),
         ),
-        in_specs=[vmem, vmem, pl.BlockSpec(memory_space=pl.ANY), vmem, vmem, vmem, vmem],
+        in_specs=[pl.BlockSpec(memory_space=pltpu.HBM)] * 7,
         out_specs=(vmem, vmem),
         scratch_shapes=[
+            pltpu.VMEM(latent_feat.shape, BF16),
+            pltpu.VMEM(norm_gain.shape, F32),
+            pltpu.VMEM((3, chans), BF16),
+            pltpu.VMEM(real_frames.shape, BF16),
+            pltpu.VMEM((3, 27, depth), BF16),
+            pltpu.VMEM((9 * depth, 3 * depth2), BF16),
             pltpu.VMEM((3, 3, chans, 3 * chans), BF16),
             pltpu.VMEM((frames + 2, height + 2, width, chans), BF16),
             pltpu.VMEM((height, frames, width, 3 * chans), F32),
@@ -349,6 +382,8 @@
             pltpu.VMEM((depth, 9 * 16), BF16),
             pltpu.VMEM((3 * depth2, 9 * depth), BF16),
             pltpu.VMEM(real_frames.shape, F32),
+            dma((5,)),
+            dma((9, 3)),
             dma((3, 3)),
             dma((2, 2)),
             dma((2, 2)),
@@ -360,16 +395,16 @@
             dma((2, 8)),
         ],
         compiler_params=pltpu.CompilerParams(
-            collective_id=0, has_side_effects=True, vmem_limit_bytes=48 * 1024 * 1024
+            collective_id=0, has_side_effects=True, vmem_limit_bytes=61 * 1024 * 1024
         ),
     )(
         latent_feat,
-        norm_gain.reshape(1, chans),
+        norm_gain,
         conv_weight.reshape(3, 3, 3, chans, chans),
-        rgb_weight,
+        rgb_weight.T,
         real_frames,
-        disc_first,
-        disc_second,
+        jnp.transpose(disc_first, (2, 0, 1)),
+        jnp.transpose(disc_second, (0, 2, 1)).reshape(9, 3, depth, depth2),
     )
 
 

time: 42.7 us -> 40.7 us (0.953)
  local copies, waits for them, and re-layouts: 7.33 us -> 3.36 us
  Pallas kernels: 34.3 us -> 36.3 us
    unnamed x9 -> x2, local copies, waits for them, and re-layouts: 6.64 us -> 3.36 us
    pallas_call x1, Pallas kernels: 34.3 us -> 36.3 us  [per_device(): pl.pallas_call(functools.partial(kernel, slabs, bands), out_shape=(jax.Sh...]
    reshape x1 -> x0, local copies, waits for them, and re-layouts: 0.68 us -> none  [per_device(): norm_gain.reshape(1, chans)]
where the time goes in v2:
time: 40.7 us; the launch traced here: 40.3 us
  Pallas kernels  36.3 us (89%)
  local copies, waits for them, and re-layouts  3.36 us (8%)
  between operations  0.64 us (2%)
    pallas_call x1, Pallas kernels, per_device(): pl.pallas_call(functools.partial(kernel, slabs, bands), out_shape=(jax.Sh...  36.3 us
    unnamed x2, local copies, waits for them, and re-layouts  3.36 us

profile of v2, /device:TPU:0, one launch (start us, length us, event | category | flops | bytes accessed | tf_op | source)
XLA Modules:
  0.0 40.3 jit_solution(7894289774490542721)
XLA Ops:
  0.6 36.3 %shard_map.86 = (bf16[4,2,128,384]{3,2,1,0:T(8,128)(2,1)}, f32[4,2,128]{2,1,0:T(2,128)}) custom-call(bf16[4,2,128,384]{3,2,1,0:T(8,128)(2,1)} %lat_in.1, f32[384]{0:T(512)} %gain_in.1, bf16[3,3,3,384,384]{4,3,2,1,0:T(8,128)(2,1)} %bitcast.6, bf16[3,384]{1,0:T(4,128)(2,1)} %bitcast.9, bf16[3,4,2,128]{3,2,1,0:T(2,128)(2,1)} %real_in.1, ...), custom_call_target="tpu_custom_call" | custom-call | tf_op jit(solution)/shard_map/pallas_call | solution.py:361
  36.9 2.1 %copy.11 = bf16[4,2,128,384]{3,2,1,0:T(8,128)(2,1)} copy(bf16[4,2,128,384]{3,2,1,0:T(8,128)(2,1)} %get-tuple-element.4) | data formatting | bytes 1572864
  39.0 1.3 %copy.12 = f32[4,2,128]{2,1,0:T(2,128)} copy(f32[4,2,128]{2,1,0:T(2,128)} %get-tuple-element.5) | data formatting | bytes 8192
